TPU v7x, 512 devices: a whole 4x4x16 slice. The times are simulated.
512 devices in a mesh: section: 32 (over y, x, core), dp: 16 (over z).
Axes of the slice: x: 4, y: 4, z: 16, core: 2. Of those that a mesh axis runs over, the one named last changes fastest.
Arguments:
- activations: bfloat16 [32, 2048, 8192], P('section', 'dp'), may hold values from -6 to 6
- norm_gain: float32 [32, 8192], P('section'), may hold values from 0.25 to 1.75
- adapter_down: bfloat16 [32, 8192, 64], P('section', 'dp'), may hold values from -0.0625 to 0.0625
- adapter_up: bfloat16 [32, 8192, 64], P('section', 'dp'), may hold values from -0.0625 to 0.0625
- counts: int32 [16, 4], P('dp'), may hold values from 1 to 32, 96 in all within a row
- upstream: bfloat16 [1536, 8192], P('dp'), may hold values from -6 to 6
Outputs:
- input_grad: bfloat16 [1536, 8192], P('dp', 'section')
- grad_down: float32 [32, 8192, 64], P('section', 'dp')
- grad_up: float32 [32, 8192, 64], P('section', 'dp')
Inputs may be any that keep to these rules, and one draw needn't show every extreme that they name: Each replica's 4 counts sum to 96, and the largest of them is 32.
All inputs are finite; a program needn't handle non-finite values.
Results may differ from a plain program's by a relative error of at most 0.04.
Values may be sent and summed in bfloat16 or wider, within the bound.
A program may use at most 64 MiB of HBM per device.

v0:
```python
import jax
import jax.numpy as jnp
from jax import lax
from jax.sharding import PartitionSpec as P

BLOCK = 8


ALPHA = 2.0
EPS = 1e-05


def shifted(shard, axis, by):
    count = lax.axis_size(axis)
    pairs = [(i, i + by) for i in range(count) if 0 <= i + by < count]
    return lax.ppermute(shard, axis, pairs)


def broadcast(value, axis, source):
    kept = jnp.where(lax.axis_index(axis) == source, value, 0).astype(value.dtype)
    return lax.psum(kept, axis)


def packed_rows(events, live_rows, cap_rows):
    bounds = jnp.cumsum(events, dtype=jnp.int32)
    starts = bounds - events
    position = jnp.arange(live_rows, dtype=jnp.int32)
    member = jnp.sum(
        (position[:, None] >= bounds[None, :]).astype(jnp.int32), axis=1, dtype=jnp.int32
    )
    choose = member[:, None] == jnp.arange(events.shape[0], dtype=jnp.int32)[None, :]
    first_row = jnp.sum(jnp.where(choose, starts[None, :], 0), axis=1, dtype=jnp.int32)
    return member * cap_rows + position - first_row


def section_backward(inputs, gain_vector, adapter_lower, adapter_upper, gradient):
    values = inputs.astype(jnp.float32)
    inverse_rms = lax.rsqrt(jnp.mean(values * values, axis=-1, keepdims=True) + EPS)
    scaled = values * inverse_rms
    normed = (scaled * gain_vector).astype(jnp.bfloat16)
    lowered = (ALPHA * jnp.dot(gradient, adapter_upper, preferred_element_type=jnp.float32)).astype(
        jnp.bfloat16
    )
    back_norm = lax.dot_general(
        lowered, adapter_lower, (((1,), (1,)), ((), ())), preferred_element_type=jnp.float32
    )
    weighted = back_norm * gain_vector
    inner_term = jnp.mean(weighted * scaled, axis=-1, keepdims=True)
    next_gradient = (
        gradient.astype(jnp.float32) + inverse_rms * (weighted - scaled * inner_term)
    ).astype(jnp.bfloat16)
    return (next_gradient, normed, lowered)


def keep_block(buffer, new_block, row_start, active):
    previous = lax.dynamic_slice_in_dim(buffer, row_start, new_block.shape[0], 0)
    return lax.dynamic_update_slice_in_dim(
        buffer, jnp.where(active, new_block, previous), row_start, 0
    )


def run_chain(inputs, entering, gain_vector, adapter_lower, adapter_upper, section_index, sections):
    row_count = inputs.shape[0]
    blocks = row_count // BLOCK
    tick_count = sections + blocks - 1
    zero_wide = jnp.zeros(inputs.shape, jnp.bfloat16)
    zero_rank = jnp.zeros((row_count, adapter_lower.shape[1]), jnp.bfloat16)
    arriving = jnp.zeros((BLOCK, inputs.shape[1]), jnp.bfloat16)

    def advance(tick_index, state_tuple):
        arriving, seen, normed_all, lowered_all, leaving_all = state_tuple
        block_index = tick_index - (sections - 1 - section_index)
        active = (block_index >= 0) & (block_index < blocks)
        row_start = jnp.clip(block_index, 0, blocks - 1) * BLOCK
        incoming = lax.dynamic_slice_in_dim(entering, row_start, BLOCK, 0)
        gradient = jnp.where(section_index == sections - 1, incoming, arriving)
        input_block = lax.dynamic_slice_in_dim(inputs, row_start, BLOCK, 0)
        next_gradient, normed, lowered = section_backward(
            input_block, gain_vector, adapter_lower, adapter_upper, gradient
        )
        seen = keep_block(seen, gradient, row_start, active)
        normed_all = keep_block(normed_all, normed, row_start, active)
        lowered_all = keep_block(lowered_all, lowered, row_start, active)
        leaving_all = keep_block(leaving_all, next_gradient, row_start, active)
        arriving = shifted(next_gradient, "section", -1)
        return (arriving, seen, normed_all, lowered_all, leaving_all)

    start_state = (arriving, zero_wide, zero_wide, zero_rank, zero_wide)
    final_state = lax.fori_loop(0, tick_count, advance, start_state)
    return (final_state[1], final_state[2], final_state[3], final_state[4])


def body(activations, norm_gain, adapter_down, adapter_up, counts, upstream):
    sections = lax.axis_size("section")
    section_index = lax.axis_index("section")
    saved_inputs = activations[0]
    gain_vector = norm_gain[0]
    lower_full, upper_full = (
        lax.all_gather(adapter_down, "dp", axis=1, tiled=True),
        lax.all_gather(adapter_up, "dp", axis=1, tiled=True),
    )
    adapter_lower = lower_full[0]
    adapter_upper = upper_full[0]
    events = counts[0]
    members = events.shape[0]
    live_rows = upstream.shape[0]
    capacity = saved_inputs.shape[0] // members
    row_index = packed_rows(events, live_rows, capacity)
    entering = jnp.zeros(saved_inputs.shape, jnp.bfloat16).at[row_index].set(upstream)
    seen, normed_all, lowered_all, leaving_all = run_chain(
        saved_inputs, entering, gain_vector, adapter_lower, adapter_upper, section_index, sections
    )
    leaving = jnp.take(leaving_all, row_index, axis=0)
    projected = jnp.dot(normed_all, adapter_lower, preferred_element_type=jnp.float32).astype(
        jnp.bfloat16
    )
    local_up = (
        ALPHA
        * lax.dot_general(
            seen, projected, (((0,), (0,)), ((), ())), preferred_element_type=jnp.float32
        )
        / live_rows
    )
    local_down = (
        lax.dot_general(
            normed_all, lowered_all, (((0,), (0,)), ((), ())), preferred_element_type=jnp.float32
        )
        / live_rows
    )
    summed_down, summed_up = (
        lax.psum_scatter(
            local_down.astype(jnp.bfloat16), "dp", scatter_dimension=0, tiled=True
        ).astype(jnp.float32),
        lax.psum_scatter(
            local_up.astype(jnp.bfloat16), "dp", scatter_dimension=0, tiled=True
        ).astype(jnp.float32),
    )
    gathered = broadcast(leaving, "section", 0)
    columns = gathered.shape[1] // sections
    input_grad = lax.dynamic_slice_in_dim(gathered, section_index * columns, columns, 1)
    return (input_grad, summed_down[None], summed_up[None])


def solution(mesh):
    return jax.shard_map(
        body,
        mesh=mesh,
        in_specs=(
            P("section", "dp", None),
            P("section", None),
            P("section", "dp", None),
            P("section", "dp", None),
            P("dp", None),
            P("dp", None),
        ),
        out_specs=(P("dp", "section"), P("section", "dp", None), P("section", "dp", None)),
        check_vma=False,
    )
```

profile of v0, /device:TPU:2, one launch (start us, length us, event | category | flops | bytes accessed | tf_op | source)
XLA Modules:
  0.0 1243.5 jit_solution(2989397969150504449)
XLA Ops:
  17.4 70.9 %all-gather.5.cloned.1.call-done = bf16[1,8192,64]{2,1,0:T(8,128)(2,1)} async-done(((bf16[1,512,64]{2,1,0:T(8,128)(2,1)}), bf16[1,8192,64]{2,1,0:T(8,128)(2,1)}) %all-gather.5.cloned.1.call-update) | async-done | bytes 1048592 | tf_op jit(solution)/shard_map/all_gather | solution.py:99
  88.3 72.8 %all-gather.3.cloned.1.call-done = bf16[1,8192,64]{2,1,0:T(8,128)(2,1)} async-done(((bf16[1,512,64]{2,1,0:T(8,128)(2,1)}), bf16[1,8192,64]{2,1,0:T(8,128)(2,1)}) %all-gather.3.cloned.1.call-update) | async-done | bytes 1048592 | tf_op jit(solution)/shard_map/all_gather | solution.py:100
  164.4 766.1 %while.23 = (s32[]{:T(128)}, bf16[8,8192]{1,0:T(8,128)(2,1)S(1)}, bf16[128,8192]{1,0:T(8,128)(2,1)}, bf16[128,8192]{1,0:T(8,128)(2,1)}, bf16[128,64]{1,0:T(8,128...) while((s32[]{:T(128)}, bf16[8,8192]{1,0:T(8,128)(2,1)S(1)}, ...), condition=%wide.region_7.8_spmd, body=%wide.region_4.7_spmd.sunk | while | flops 18220564 | bytes 9380943 | solution.py:89
  352.4 6.5 collective-permute-done
  369.2 6.5 collective-permute-done
  386.0 6.5 collective-permute-done
  419.6 6.5 collective-permute-done
  436.4 6.5 collective-permute-done
  453.2 6.5 collective-permute-done
  520.5 6.5 collective-permute-done
  537.3 6.5 collective-permute-done
  554.1 6.5 collective-permute-done
  621.3 6.5 collective-permute-done
  654.9 6.5 collective-permute-done
  688.5 6.5 collective-permute-done
  705.3 6.5 collective-permute-done
  738.9 6.5 collective-permute-done
  789.3 6.5 collective-permute-done
  839.6 6.6 collective-permute-done
  873.3 6.6 collective-permute-done
  890.3 6.5 collective-permute-done
  944.4 146.6 %all-reduce.2.cloned.1.call-done = bf16[96,8192]{1,0:T(8,128)(2,1)} async-done(((bf16[96,8192]{1,0:T(8,128)(2,1)}), bf16[96,8192]{1,0:T(8,128)(2,1)}) %all-reduce.2.cloned.1.call-update) | async-done | bytes 1572880 | tf_op jit(solution)/shard_map/psum | solution.py:21
  1092.4 72.3 %reduce-scatter.5.cloned.1.call-done = bf16[512,64]{0,1:T(8,128)(2,1)} async-done(((bf16[8192,64]{0,1:T(8,128)(2,1)}), bf16[512,64]{0,1:T(8,128)(2,1)}) %reduce-scatter.5.cloned.1.call-update) | async-done | bytes 65552 | tf_op jit(solution)/shard_map/reduce_scatter | solution.py:134
  1166.2 69.3 %reduce-scatter.3.cloned.1.call-done = bf16[512,64]{0,1:T(8,128)(2,1)} async-done(((bf16[8192,64]{0,1:T(8,128)(2,1)}), bf16[512,64]{0,1:T(8,128)(2,1)}) %reduce-scatter.3.cloned.1.call-update) | async-done | bytes 65552 | tf_op jit(solution)/shard_map/reduce_scatter | solution.py:131
  (535 shorter events, 678.9 us)
Async XLA Ops:
  7.2 81.1 %all-gather.5.cloned.1.call-start = ((), (), s32[]{:S(2)}) async-start(), calls=%async_computation.3 | async-start | bytes 2228224 | tf_op jit(solution)/shard_map/all_gather | solution.py:99
  8.8 152.2 %all-gather.3.cloned.1.call-start = ((), (), s32[]{:S(2)}) async-start(), calls=%async_computation.2 | async-start | bytes 2228224 | tf_op jit(solution)/shard_map/all_gather | solution.py:100
  10.5 1080.4 %all-reduce.2.cloned.1.call-start = ((), (), s32[]{:S(2)}) async-start(), calls=%async_computation.4 | async-start | bytes 3145728 | tf_op jit(solution)/shard_map/psum | solution.py:21
  333.7 8.4 collective-permute-start
  350.5 8.4 collective-permute-start
  367.3 8.4 collective-permute-start
  384.1 8.4 collective-permute-start
  417.7 8.4 collective-permute-start
  434.5 8.4 collective-permute-start
  451.3 8.4 collective-permute-start
  518.5 8.4 collective-permute-start
  535.3 8.4 collective-permute-start
  552.2 8.4 collective-permute-start
  619.4 8.4 collective-permute-start
  652.9 8.4 collective-permute-start
  686.5 8.4 collective-permute-start
  703.4 8.4 collective-permute-start
  737.0 8.4 collective-permute-start
  787.4 8.4 collective-permute-start
  837.7 8.5 collective-permute-start
  871.4 8.5 collective-permute-start
  888.4 8.4 collective-permute-start
  936.2 228.5 %reduce-scatter.5.cloned.1.call-start = ((), (), s32[]{:S(2)}) async-start(), calls=%async_computation.6 | async-start | bytes 1114112 | tf_op jit(solution)/shard_map/reduce_scatter | solution.py:134
  941.2 294.3 %reduce-scatter.3.cloned.1.call-start = ((), (), s32[]{:S(2)}) async-start(), calls=%async_computation.5 | async-start | bytes 1114112 | tf_op jit(solution)/shard_map/reduce_scatter | solution.py:131
  (77 other events, 394.6 us)
Sparse Core Ops, SparseCore 0:
  10.7 77.5 all-gather.4
  90.9 70.0 all-gather.2
  936.3 154.5 all-reduce.1
  1093.8 70.8 reduce-scatter.4
  1167.3 68.0 reduce-scatter.2
where the time goes:
time: 1250 us; the launch traced here: 1240 us
  waiting for transfers between devices  692 us (55%)
  other arithmetic  230 us (18%)
  matrix products  180 us (14%)
  starting transfers between devices  109 us (9%)
  local copies, waits for them, and re-layouts  16.1 us (1%)
  between operations  13.8 us (1%)
    ppermute x47, waiting for transfers between devices, shifted(): return lax.ppermute(shard, axis, pairs)  261 us
    dynamic_update_slice x94, other arithmetic, keep_block(): lax.dynamic_update_slice_in_dim(buffer, jnp.where(active, new_block, prev...  171 us
    psum x1, waiting for transfers between devices, broadcast(): return lax.psum(kept, axis)  147 us
    ppermute x47, starting transfers between devices, shifted(): return lax.ppermute(shard, axis, pairs)  109 us
    dot_general x47, matrix products, section_backward(): jnp.dot(gradient, adapter_upper, preferred_element_type=jnp.float32)  92.9 us
    dot_general x47, matrix products, section_backward(): lax.dot_general(lowered, adapter_lower, (((1,), (1,)), ((), ())), preferr...  78.8 us
    all_gather x1, waiting for transfers between devices, body(): lax.all_gather(adapter_up, 'dp', axis=1, tiled=True)  72.8 us
    reduce_scatter x1, waiting for transfers between devices, body(): lax.psum_scatter(local_up.astype(jnp.bfloat16), 'dp', scatter_dimension=0...  72.3 us
  transfers between devices with their start and end apart: 52, of which 52 were waited for; matrix products, arithmetic and copies ran while one was open for 2% of the time, Pallas kernels for 0%

commit v1 on v0

v1 whole, which is shorter than its diff:
```python
import functools

import jax
import jax.numpy as jnp
from jax import lax
from jax.experimental import pallas as pl
from jax.experimental.pallas import tpu as pltpu
from jax.sharding import PartitionSpec as P

ALPHA = 2.0
EPS = 1e-05
QUARTERS = 4
TILE = 16
ROWS = TILE // QUARTERS
MESH = pl.DeviceIdType.MESH
F32 = jnp.float32
BF16 = jnp.bfloat16


def iota(shape, dim):
    return lax.broadcasted_iota(jnp.int32, shape, dim)


def quarter_mask(shape, rank):
    quarter = (iota(shape, 0) // ROWS) % QUARTERS
    return quarter == iota(shape, 1) // rank


def dot(a, b, dims=((1,), (0,)), **kw):
    return lax.dot_general(a, b, (dims, ((), ())), preferred_element_type=F32, **kw)


def kernel(
    n_sec, n_dp, cap,
    counts_ref, x_hbm, gain_ref, down_ref, up_ref, upstream_hbm,
    input_grad_ref, grad_down_ref, grad_up_ref,
    raw, nat, landed, pieces, weight_up, weight_down, held_x, row_scale, coef_rank, projected_all,
    gin, gout, lowered_all, part_up, part_down, slots,
    load_sem, gather_send, gather_recv, chain_send, chain_recv, final_send, final_recv, ring_send, ring_recv,
):
    sec, me = lax.axis_index("section"), lax.axis_index("dp")
    right, left = lax.rem(me + 1, n_dp), lax.rem(me + n_dp - 1, n_dp)
    live, width = nat.shape
    blocks = live // ROWS
    packed = blocks * TILE
    span = width // QUARTERS
    shard, rank = down_ref.shape[1], down_ref.shape[2]
    per_quarter = span // shard
    columns = width // n_sec
    wide = QUARTERS * rank

    load_x = pltpu.make_async_copy(x_hbm.at[0], raw, load_sem.at[0])
    load_x.start()
    load_up = pltpu.make_async_copy(upstream_hbm, nat, load_sem.at[1])

    @pl.when(sec == n_sec - 1)
    def _():
        load_up.start()

    barrier = pltpu.get_barrier_semaphore()
    for side in (left, right):
        pl.semaphore_signal(barrier, inc=1, device_id={"dp": side}, device_id_type=MESH)

    @pl.when(sec > 0)
    def _():
        pl.semaphore_signal(barrier, inc=1, device_id={"section": sec - 1}, device_id_type=MESH)

    @pl.when(sec < n_sec - 1)
    def _():
        pl.semaphore_signal(barrier, inc=1, device_id={"section": sec + 1}, device_id_type=MESH)

    @pl.when(sec > 1)
    def _():
        pl.semaphore_signal(barrier, inc=1, device_id={"section": 0}, device_id_type=MESH)

    @pl.when(sec == 0)
    def _():
        @pl.loop(2, n_sec)
        def _(c):
            pl.semaphore_signal(barrier, inc=1, device_id={"section": c}, device_id_type=MESH)

    my_gain = gain_ref[:, pl.ds(pl.multiple_of(me * shard, shard), shard)]
    pieces[me, 0:rank, :] = up_ref[0].astype(F32).T.astype(BF16)
    pieces[me, rank:2 * rank, :] = (down_ref[0].astype(F32).T * my_gain).astype(BF16)

    @pl.when(sec == 0)
    def _():
        pl.semaphore_wait(barrier, 3 + n_sec - 2)

    @pl.when(sec == 1)
    def _():
        pl.semaphore_wait(barrier, 4)

    @pl.when((sec > 1) & (sec < n_sec - 1))
    def _():
        pl.semaphore_wait(barrier, 5)

    @pl.when(sec == n_sec - 1)
    def _():
        pl.semaphore_wait(barrier, 4)

    def gather_copy(slot, half, way):
        part = pieces.at[slot, pl.ds(half * rank, rank)]
        return pltpu.make_async_remote_copy(
            src_ref=part,
            dst_ref=part,
            send_sem=gather_send.at[way, half, slot],
            recv_sem=gather_recv.at[half, slot],
            device_id={"dp": right if way == 0 else left},
            device_id_type=MESH,
        )

    far = n_dp // 2
    reach = {(0, 0): far, (0, 1): far - 1, (1, 0): far - 1, (1, 1): far}
    for half in (0, 1):
        for way in (0, 1):
            gather_copy(me, half, way).start()

    load_x.wait()
    raw_rows = raw.shape[0]
    prep_rows = raw_rows // far
    scales = []
    for hop in range(1, far + 1):
        for half in (0, 1):
            for way in (0, 1):
                if hop <= reach[way, half]:
                    slot = lax.rem(me + (n_dp - hop if way == 0 else hop), n_dp)
                    here = gather_copy(slot, half, way)
                    here.wait_recv()
                    if hop < reach[way, half]:
                        here.start()
        rows = pl.ds((hop - 1) * prep_rows, prep_rows)
        values = raw[rows, :].astype(F32)
        inverse = lax.rsqrt(jnp.mean(values * values, axis=-1, keepdims=True) + EPS)
        raw[rows, :] = (values * inverse).astype(BF16)
        scales.append(inverse)
    inverse_all = jnp.broadcast_to(jnp.concatenate(scales, axis=0), (raw_rows, 128))

    line = iota((packed, raw_rows), 0)
    position = (line // TILE) * ROWS + lax.rem(line, ROWS)
    source = position
    bound = jnp.int32(0)
    members = counts_ref.shape[1]
    for member in range(members - 1):
        count = counts_ref[0, member]
        bound = bound + count
        source = source + jnp.where(position >= bound, cap - count, 0)
    chosen = source == iota((packed, raw_rows), 1)
    row_scale[...] = dot(chosen.astype(F32), inverse_all, precision=lax.Precision.HIGHEST).reshape(
        blocks, TILE, 128
    )
    quarter = (line // ROWS) % QUARTERS
    picks = [(chosen & (quarter == q)).astype(BF16) for q in range(QUARTERS)]
    for n in range(per_quarter):
        cols = slice(n * shard, (n + 1) * shard)
        total = jnp.zeros((packed, shard), F32)
        for q in range(QUARTERS):
            total += dot(picks[q], raw[:, q * span + n * shard:q * span + (n + 1) * shard])
        held_x[:, :, cols] = total.astype(BF16).reshape(blocks, TILE, shard)

    @pl.when(sec == n_sec - 1)
    def _():
        load_up.wait()
        line = iota((packed, live), 0)
        position = (line // TILE) * ROWS + lax.rem(line, ROWS)
        chosen = position == iota((packed, live), 1)
        quarter = (line // ROWS) % QUARTERS
        for n in range(per_quarter):
            cols = slice(n * shard, (n + 1) * shard)
            total = jnp.zeros((packed, shard), F32)
            for q in range(QUARTERS):
                pick = (chosen & (quarter == q)).astype(BF16)
                total += dot(pick, nat[:, q * span + n * shard:q * span + (n + 1) * shard])
            gin[:, :, cols] = total.astype(BF16).reshape(blocks, TILE, shard)

    for n in range(per_quarter):
        cols = slice(n * shard, (n + 1) * shard)
        stack = jnp.concatenate([pieces[q * per_quarter + n, 0:rank, :] for q in range(QUARTERS)], axis=0)
        weight_up[cols, :] = stack.astype(F32).T.astype(BF16)
        for q in range(QUARTERS):
            weight_down[q * rank:(q + 1) * rank, cols] = pieces[q * per_quarter + n, rank:2 * rank, :]

    def fold(product):
        pair = product[:, 0:128] + product[:, 128:256]
        return pair + pltpu.roll(pair, 64, 1)

    product = dot(held_x[...].reshape(packed, span), weight_down[...], ((1,), (1,)))
    product = jnp.where(quarter_mask((packed, wide), rank), product, 0.0)
    folded = fold(product).reshape(blocks, TILE, 128)
    folded = folded[:, 0:8, :] + folded[:, 8:16, :]
    folded = (folded + pltpu.roll(folded, 4, 1)).astype(BF16).astype(F32)
    lane = lax.broadcasted_iota(jnp.int32, folded.shape, 2)
    coef_rank[...] = jnp.where(lane < rank, folded * (1.0 / width), 0.0)
    tall = jnp.concatenate([folded, folded], axis=1)
    tall = jnp.concatenate([tall, tall], axis=2).reshape(packed, wide)
    projected_all[...] = jnp.where(quarter_mask((packed, wide), rank), tall, 0.0).astype(BF16)

    def chain_copy(block):
        return pltpu.make_async_remote_copy(
            src_ref=gout.at[block],
            dst_ref=gin.at[block],
            send_sem=chain_send.at[block],
            recv_sem=chain_recv.at[block],
            device_id={"section": sec - 1},
            device_id_type=MESH,
        )

    group = 32
    group_blocks = group // ROWS

    def final_copy(k, c):
        rows = pl.ds(pl.multiple_of(k * group, group), group)
        return pltpu.make_async_remote_copy(
            src_ref=nat.at[rows, pl.ds(pl.multiple_of(c * columns, columns), columns)],
            dst_ref=landed.at[rows],
            send_sem=final_send.at[k, c],
            recv_sem=final_recv.at[k],
            device_id={"section": c},
            device_id_type=MESH,
        )

    mask = quarter_mask((TILE, wide), rank)

    def spread(rows8):
        tall = jnp.concatenate([rows8, rows8], axis=0)
        tall = jnp.concatenate([tall, tall], axis=1)
        return jnp.where(mask, tall, 0.0).astype(BF16)

    @pl.loop(0, blocks)
    def _(block):
        @pl.when(sec < n_sec - 1)
        def _():
            pltpu.make_async_remote_copy(
                src_ref=gout.at[block],
                dst_ref=gin.at[block],
                send_sem=chain_send.at[block],
                recv_sem=chain_recv.at[block],
                device_id={"section": lax.rem(sec + n_sec - 1, n_sec)},
                device_id_type=MESH,
            ).wait_recv()

        product = jnp.where(mask, dot(gin[block], weight_up[...]), 0.0)
        pair = fold(product)
        pair = pair[0:8, :] + pair[8:16, :]
        lowered = ((pair + pltpu.roll(pair, 4, 0)) * ALPHA).astype(BF16).astype(F32)
        scaled = lowered * row_scale[block, 0:8, :]
        coef = jnp.sum(scaled * coef_rank[block], axis=-1, keepdims=True)
        coef = jnp.concatenate([coef, coef], axis=0)
        scaled = spread(scaled)
        for n in range(per_quarter):
            cols = slice(n * shard, (n + 1) * shard)
            back = dot(scaled, weight_down[:, cols])
            fresh = gin[block, :, cols].astype(F32) + (back - held_x[block, :, cols].astype(F32) * coef)
            gout[block, :, cols] = fresh.astype(BF16)

        @pl.when(sec > 0)
        def _():
            chain_copy(block).start()

        lowered_all[block] = spread(lowered)

        @pl.when((sec == 0) & (lax.rem(block, group_blocks) == group_blocks - 1))
        def _():
            k = block // group_blocks
            done = gout[pl.ds(k * group_blocks, group_blocks)].reshape(group_blocks * TILE, span)
            shape = (group, group_blocks * TILE)
            row = iota(shape, 0)
            for q in range(QUARTERS):
                want = (row // ROWS) * TILE + q * ROWS + lax.rem(row, ROWS)
                pick = (want == iota(shape, 1)).astype(BF16)
                rows = pl.ds(pl.multiple_of(k * group, group), group)
                nat[rows, q * span:(q + 1) * span] = dot(pick, done).astype(BF16)

            @pl.loop(1, n_sec)
            def _(c):
                final_copy(k, c).start()

    low_t = lowered_all[...].reshape(packed, wide).astype(F32).T.astype(BF16)
    pro_t = projected_all[...].astype(F32).T.astype(BF16)
    for n in range(per_quarter):
        cols = slice(n * shard, (n + 1) * shard)
        part_up[:, cols] = dot(pro_t, gin[:, :, cols].reshape(packed, shard)) * (ALPHA / live)
        part_down[:, cols] = dot(low_t, held_x[:, :, cols].reshape(packed, shard)) * (1.0 / live)

    half_rank = rank // 2
    parts = (part_up, part_down)

    def own(kind, way, piece):
        start = (piece // per_quarter) * rank + way * half_rank
        rows = pl.ds(pl.multiple_of(start, half_rank), half_rank)
        cols = pl.ds(pl.multiple_of(lax.rem(piece, per_quarter) * shard, shard), shard)
        return parts[kind][rows, cols]

    def ring_copy(kind, way, step):
        return pltpu.make_async_remote_copy(
            src_ref=slots.at[kind, way, step],
            dst_ref=slots.at[kind, way, step + 1],
            send_sem=ring_send.at[kind, way, step],
            recv_sem=ring_recv.at[kind, way, step + 1],
            device_id={"dp": right if way == 0 else left},
            device_id_type=MESH,
        )

    streams = [(kind, way) for kind in (0, 1) for way in (0, 1)]

    def piece_at(way, step):
        if way == 0:
            return lax.rem(me + 2 * n_dp - 1 - step, n_dp)
        return lax.rem(me + 1 + step, n_dp)

    for kind, way in streams:
        slots[kind, way, 0] = own(kind, way, piece_at(way, 0)).astype(BF16)
        ring_copy(kind, way, 0).start()

    @pl.loop(1, n_dp - 1)
    def _(step):
        for kind, way in streams:
            ring_copy(kind, way, step - 1).wait_recv()
            total = slots[kind, way, step].astype(F32) + own(kind, way, piece_at(way, step))
            slots[kind, way, step] = total.astype(BF16)
            ring_copy(kind, way, step).start()

    last = n_dp - 1
    totals = []
    for kind, way in streams:
        ring_copy(kind, way, last - 1).wait_recv()
        totals.append(slots[kind, way, last].astype(F32) + own(kind, way, me))
    grad_up_ref[0] = jnp.concatenate(totals[0:2], axis=0).T
    grad_down_ref[0] = (jnp.concatenate(totals[2:4], axis=0) * my_gain).T

    groups = live // group

    @pl.when(sec == 0)
    def _():
        input_grad_ref[...] = nat[:, 0:columns]

        @pl.loop(0, groups)
        def _(k):
            @pl.loop(1, n_sec)
            def _(c):
                final_copy(k, c).wait_send()

    @pl.when(sec > 0)
    def _():
        @pl.loop(0, groups)
        def _(k):
            final_copy(k, sec).wait_recv()

        input_grad_ref[...] = landed[...]

        @pl.loop(0, blocks)
        def _(block):
            chain_copy(block).wait_send()

    for half in (0, 1):
        for way in (0, 1):
            for hop in range(reach[way, half]):
                slot = lax.rem(me + (n_dp - hop if way == 0 else hop), n_dp)
                gather_copy(slot, half, way).wait_send()

    @pl.loop(0, n_dp - 1)
    def _(step):
        for kind, way in streams:
            ring_copy(kind, way, step).wait_send()


def solution(mesh):
    n_sec, n_dp = mesh.shape["section"], mesh.shape["dp"]

    def body(activations, norm_gain, adapter_down, adapter_up, counts, upstream):
        raw_rows, width = activations.shape[1:]
        shard, rank = adapter_down.shape[1:]
        live = upstream.shape[0]
        cap = raw_rows // counts.shape[1]
        blocks = live // ROWS
        packed = blocks * TILE
        span = width // QUARTERS
        wide = QUARTERS * rank
        columns = width // n_sec
        groups = live // 32
        dma = pltpu.SemaphoreType.DMA
        vmem = pl.BlockSpec(memory_space=pltpu.VMEM)
        hbm = pl.BlockSpec(memory_space=pl.ANY)
        return pl.pallas_call(
            functools.partial(kernel, n_sec, n_dp, cap),
            out_shape=(
                jax.ShapeDtypeStruct((live, columns), BF16),
                jax.ShapeDtypeStruct((1, shard, rank), F32),
                jax.ShapeDtypeStruct((1, shard, rank), F32),
            ),
            in_specs=[pl.BlockSpec(memory_space=pltpu.SMEM), hbm, vmem, vmem, vmem, hbm],
            out_specs=(vmem, vmem, vmem),
            scratch_shapes=[
                pltpu.VMEM((raw_rows, width), BF16),
                pltpu.VMEM((live, width), BF16),
                pltpu.VMEM((live, columns), BF16),
                pltpu.VMEM((n_dp, 2 * rank, shard), BF16),
                pltpu.VMEM((span, wide), BF16),
                pltpu.VMEM((wide, span), BF16),
                pltpu.VMEM((blocks, TILE, span), BF16),
                pltpu.VMEM((blocks, TILE, 128), F32),
                pltpu.VMEM((blocks, 8, 128), F32),
                pltpu.VMEM((packed, wide), BF16),
                pltpu.VMEM((blocks, TILE, span), BF16),
                pltpu.VMEM((blocks, TILE, span), BF16),
                pltpu.VMEM((blocks, TILE, wide), BF16),
                pltpu.VMEM((wide, span), F32),
                pltpu.VMEM((wide, span), F32),
                pltpu.VMEM((2, 2, n_dp, rank // 2, shard), BF16),
                dma((2,)),
                dma((2, 2, n_dp)),
                dma((2, n_dp)),
                dma((blocks,)),
                dma((blocks,)),
                dma((groups, n_sec)),
                dma((groups,)),
                dma((2, 2, n_dp)),
                dma((2, 2, n_dp)),
            ],
            compiler_params=pltpu.CompilerParams(
                collective_id=0, has_side_effects=True, vmem_limit_bytes=48 * 1024 * 1024
            ),
        )(counts, activations, norm_gain, adapter_down, adapter_up, upstream)

    return jax.shard_map(
        body,
        mesh=mesh,
        in_specs=(
            P("section", "dp", None),
            P("section", None),
            P("section", "dp", None),
            P("section", "dp", None),
            P("dp", None),
            P("dp", None),
        ),
        out_specs=(P("dp", "section"), P("section", "dp", None), P("section", "dp", None)),
        check_vma=False,
    )
```

time: 1250 us -> 219 us (0.18)
  the two profiles are of different devices: /device:TPU:2 before, /device:TPU:32 now
where the time goes in v1:
time: 219 us; the launch traced here: 218 us
  Pallas kernels  209 us (95%)
  local copies, waits for them, and re-layouts  8.49 us (4%)
    pallas_call x1, Pallas kernels, body(): pl.pallas_call(functools.partial(kernel, n_sec, n_dp, cap), out_shape=(ja...  209 us
    unnamed x11, local copies, waits for them, and re-layouts  6.94 us

profile of v1, /device:TPU:32, one launch (start us, length us, event | category | flops | bytes accessed | tf_op | source)
XLA Modules:
  0.0 218.5 jit_solution(3625566092345305864)
XLA Ops:
  0.6 1.0 copy.9.down_ref
  1.6 1.0 copy.10.up_ref
  2.6 0.0 copy-start
  2.6 1.6 copy-done
  4.2 0.0 copy-start.1
  4.2 1.4 copy-done.1
  5.6 0.0 copy-start.2
  5.6 0.8 copy-done.2
  6.3 0.0 copy-start.3
  6.3 0.7 copy-done.3
  7.0 209.3 %shard_map.85 = (bf16[96,256]{1,0:T(8,128)(2,1)S(1)}, f32[1,512,64]{2,1,0:T(8,128)S(1)}, f32[1,512,64]{2,1,0:T(8,128)S(1)}) custom-call(s32[1,4]{1,0:T(1,128)S(1)} %copy-done.3, bf16[1,128,8192]{2,1,0:T(8,128)(2,1)S(1)} %copy-done, f32[1,8192]{1,0:T(1,128)S(1)} %copy-done.2, bf16[1,512,64]{2,1,0:T(8,128)(2,1)S(1)} %copy.9.down_ref, ...), custom_call_target="tpu_custom_call" | custom-call | tf_op jit(solution)/shard_map/pallas_call | solution.py:384
  216.3 0.8 copy.11
  217.1 0.8 copy.12
  217.8 0.6 copy.14
Async XLA Ops:
  2.6 1.6 copy-start
  4.2 1.4 copy-start.1
  5.6 0.8 copy-start.2
  6.3 0.7 copy-start.3

commit v2 on v1

--- a/solution.py
+++ b/solution.py
@@ -32,9 +32,9 @@
 
 def kernel(
     n_sec, n_dp, cap,
-    counts_ref, x_hbm, gain_ref, down_ref, up_ref, upstream_hbm,
+    counts_hbm, x_hbm, gain_hbm, down_hbm, up_hbm, upstream_hbm,
     input_grad_ref, grad_down_ref, grad_up_ref,
-    raw, nat, landed, pieces, weight_up, weight_down, held_x, row_scale, coef_rank, projected_all,
+    counts_ref, gain_ref, own_maps, raw, nat, landed, pieces, weight_up, weight_down, held_x, row_scale, coef_rank, projected_all,
     gin, gout, lowered_all, part_up, part_down, slots,
     load_sem, gather_send, gather_recv, chain_send, chain_recv, final_send, final_recv, ring_send, ring_recv,
 ):
@@ -44,11 +44,19 @@
     blocks = live // ROWS
     packed = blocks * TILE
     span = width // QUARTERS
-    shard, rank = down_ref.shape[1], down_ref.shape[2]
+    rank, shard = down_hbm.shape[1:]
     per_quarter = span // shard
     columns = width // n_sec
     wide = QUARTERS * rank
 
+    small = [
+        pltpu.make_async_copy(up_hbm, own_maps.at[pl.ds(0, 1)], load_sem.at[2]),
+        pltpu.make_async_copy(down_hbm, own_maps.at[pl.ds(1, 1)], load_sem.at[3]),
+        pltpu.make_async_copy(gain_hbm, gain_ref, load_sem.at[4]),
+        pltpu.make_async_copy(counts_hbm, counts_ref, load_sem.at[5]),
+    ]
+    for load in small:
+        load.start()
     load_x = pltpu.make_async_copy(x_hbm.at[0], raw, load_sem.at[0])
     load_x.start()
     load_up = pltpu.make_async_copy(upstream_hbm, nat, load_sem.at[1])
@@ -79,9 +87,11 @@
         def _(c):
             pl.semaphore_signal(barrier, inc=1, device_id={"section": c}, device_id_type=MESH)
 
+    for load in small:
+        load.wait()
     my_gain = gain_ref[:, pl.ds(pl.multiple_of(me * shard, shard), shard)]
-    pieces[me, 0:rank, :] = up_ref[0].astype(F32).T.astype(BF16)
-    pieces[me, rank:2 * rank, :] = (down_ref[0].astype(F32).T * my_gain).astype(BF16)
+    pieces[me, 0:rank, :] = own_maps[0]
+    pieces[me, rank:2 * rank, :] = (own_maps[1].astype(F32) * my_gain).astype(BF16)
 
     @pl.when(sec == 0)
     def _():
@@ -118,8 +128,55 @@
 
     load_x.wait()
     raw_rows = raw.shape[0]
-    prep_rows = raw_rows // far
-    scales = []
+    members = counts_ref.shape[1]
+
+    def place(slot):
+        rows = pl.ds(pl.multiple_of((slot // per_quarter) * rank, rank), rank)
+        cols = pl.ds(pl.multiple_of(lax.rem(slot, per_quarter) * shard, shard), shard)
+        weight_down[rows, cols] = pieces[slot, rank:2 * rank, :]
+
+    def sources(shape):
+        line = iota(shape, 0)
+        position = (line // TILE) * ROWS + lax.rem(line, ROWS)
+        source = position
+        bound = jnp.int32(0)
+        for member in range(members - 1):
+            count = counts_ref[0, member]
+            bound = bound + count
+            source = source + jnp.where(position >= bound, cap - count, 0)
+        return source == iota(shape, 1), (line // ROWS) % QUARTERS
+
+    prep_rows = 16
+    norm_jobs = raw_rows // prep_rows
+    inverses = []
+
+    def work(job):
+        if job < norm_jobs:
+            rows = pl.ds(job * prep_rows, prep_rows)
+            values = raw[rows, :].astype(F32)
+            inverse = lax.rsqrt(jnp.mean(values * values, axis=-1, keepdims=True) + EPS)
+            raw[rows, :] = (values * inverse).astype(BF16)
+            inverses.append(inverse)
+        elif job == norm_jobs:
+            chosen, _ = sources((packed, raw_rows))
+            inverse_all = jnp.broadcast_to(jnp.concatenate(inverses, axis=0), (raw_rows, 128))
+            row_scale[...] = dot(
+                chosen.astype(F32), inverse_all, precision=lax.Precision.HIGHEST
+            ).reshape(blocks, TILE, 128)
+        elif job <= norm_jobs + per_quarter:
+            n = job - norm_jobs - 1
+            chosen, quarter = sources((packed, raw_rows))
+            total = jnp.zeros((packed, shard), F32)
+            for q in range(QUARTERS):
+                pick = (chosen & (quarter == q)).astype(BF16)
+                total += dot(pick, raw[:, q * span + n * shard:q * span + (n + 1) * shard])
+            held_x[:, :, n * shard:(n + 1) * shard] = total.astype(BF16).reshape(blocks, TILE, shard)
+
+    jobs = norm_jobs + 1 + per_quarter
+    done = 0
+    turns = 2 * far
+    turn = 0
+    place(me)
     for hop in range(1, far + 1):
         for half in (0, 1):
             for way in (0, 1):
@@ -129,34 +186,12 @@
                     here.wait_recv()
                     if hop < reach[way, half]:
                         here.start()
-        rows = pl.ds((hop - 1) * prep_rows, prep_rows)
-        values = raw[rows, :].astype(F32)
-        inverse = lax.rsqrt(jnp.mean(values * values, axis=-1, keepdims=True) + EPS)
-        raw[rows, :] = (values * inverse).astype(BF16)
-        scales.append(inverse)
-    inverse_all = jnp.broadcast_to(jnp.concatenate(scales, axis=0), (raw_rows, 128))
-
-    line = iota((packed, raw_rows), 0)
-    position = (line // TILE) * ROWS + lax.rem(line, ROWS)
-    source = position
-    bound = jnp.int32(0)
-    members = counts_ref.shape[1]
-    for member in range(members - 1):
-        count = counts_ref[0, member]
-        bound = bound + count
-        source = source + jnp.where(position >= bound, cap - count, 0)
-    chosen = source == iota((packed, raw_rows), 1)
-    row_scale[...] = dot(chosen.astype(F32), inverse_all, precision=lax.Precision.HIGHEST).reshape(
-        blocks, TILE, 128
-    )
-    quarter = (line // ROWS) % QUARTERS
-    picks = [(chosen & (quarter == q)).astype(BF16) for q in range(QUARTERS)]
-    for n in range(per_quarter):
-        cols = slice(n * shard, (n + 1) * shard)
-        total = jnp.zeros((packed, shard), F32)
-        for q in range(QUARTERS):
-            total += dot(picks[q], raw[:, q * span + n * shard:q * span + (n + 1) * shard])
-        held_x[:, :, cols] = total.astype(BF16).reshape(blocks, TILE, shard)
+                    if half == 1:
+                        place(slot)
+            turn += 1
+            while done * turns < jobs * turn:
+                work(done)
+                done += 1
 
     @pl.when(sec == n_sec - 1)
     def _():
@@ -176,9 +211,7 @@
     for n in range(per_quarter):
         cols = slice(n * shard, (n + 1) * shard)
         stack = jnp.concatenate([pieces[q * per_quarter + n, 0:rank, :] for q in range(QUARTERS)], axis=0)
-        weight_up[cols, :] = stack.astype(F32).T.astype(BF16)
-        for q in range(QUARTERS):
-            weight_down[q * rank:(q + 1) * rank, cols] = pieces[q * per_quarter + n, rank:2 * rank, :]
+        weight_up[cols, :] = stack.T
 
     def fold(product):
         pair = product[:, 0:128] + product[:, 128:256]
@@ -277,56 +310,76 @@
 
     low_t = lowered_all[...].reshape(packed, wide).astype(F32).T.astype(BF16)
     pro_t = projected_all[...].astype(F32).T.astype(BF16)
-    for n in range(per_quarter):
-        cols = slice(n * shard, (n + 1) * shard)
-        part_up[:, cols] = dot(pro_t, gin[:, :, cols].reshape(packed, shard)) * (ALPHA / live)
-        part_down[:, cols] = dot(low_t, held_x[:, :, cols].reshape(packed, shard)) * (1.0 / live)
-
     half_rank = rank // 2
     parts = (part_up, part_down)
 
-    def own(kind, way, piece):
-        start = (piece // per_quarter) * rank + way * half_rank
+    def own(kind, half, piece):
+        start = (piece // per_quarter) * rank + half * half_rank
         rows = pl.ds(pl.multiple_of(start, half_rank), half_rank)
         cols = pl.ds(pl.multiple_of(lax.rem(piece, per_quarter) * shard, shard), shard)
         return parts[kind][rows, cols]
 
-    def ring_copy(kind, way, step):
+    def ring_copy(kind, way, half, step):
         return pltpu.make_async_remote_copy(
-            src_ref=slots.at[kind, way, step],
-            dst_ref=slots.at[kind, way, step + 1],
-            send_sem=ring_send.at[kind, way, step],
-            recv_sem=ring_recv.at[kind, way, step + 1],
+            src_ref=slots.at[kind, way, half, step],
+            dst_ref=slots.at[kind, way, half, step + 1],
+            send_sem=ring_send.at[kind, way, half, step],
+            recv_sem=ring_recv.at[kind, way, half, step + 1],
             device_id={"dp": right if way == 0 else left},
             device_id_type=MESH,
         )
 
-    streams = [(kind, way) for kind in (0, 1) for way in (0, 1)]
-
-    def piece_at(way, step):
-        if way == 0:
-            return lax.rem(me + 2 * n_dp - 1 - step, n_dp)
-        return lax.rem(me + 1 + step, n_dp)
-
-    for kind, way in streams:
-        slots[kind, way, 0] = own(kind, way, piece_at(way, 0)).astype(BF16)
-        ring_copy(kind, way, 0).start()
-
-    @pl.loop(1, n_dp - 1)
+    def target(kind, way, step):
+        distance = reach[way, kind] - step
+        return lax.rem(me + (distance if way == 0 else n_dp - distance), n_dp)
+
+    def partial(offset):
+        cols = pl.ds(pl.multiple_of(lax.rem(me + far + per_quarter + offset, per_quarter) * shard, shard), shard)
+        part_up[:, cols] = dot(pro_t, gin[:, :, cols].reshape(packed, shard)) * (ALPHA / live)
+        part_down[:, cols] = dot(low_t, held_x[:, :, cols].reshape(packed, shard)) * (1.0 / live)
+
+    def begin(kind, way):
+        for half in (0, 1):
+            slots[kind, way, half, 0] = own(kind, half, target(kind, way, 0)).astype(BF16)
+            ring_copy(kind, way, half, 0).start()
+
+    def forward(kind, way, step):
+        for half in (0, 1):
+            ring_copy(kind, way, half, step - 1).wait_recv()
+            total = slots[kind, way, half, step].astype(F32) + own(kind, half, target(kind, way, step))
+            slots[kind, way, half, step] = total.astype(BF16)
+            ring_copy(kind, way, half, step).start()
+
+    partial(0)
+    begin(0, 0)
+    begin(1, 1)
+    partial(-1)
+    begin(1, 0)
+    partial(1)
+    begin(0, 1)
+    partial(2)
+    streams = [(0, 0), (1, 1), (1, 0), (0, 1)]
+
+    @pl.loop(1, far - 1)
     def _(step):
         for kind, way in streams:
-            ring_copy(kind, way, step - 1).wait_recv()
-            total = slots[kind, way, step].astype(F32) + own(kind, way, piece_at(way, step))
-            slots[kind, way, step] = total.astype(BF16)
-            ring_copy(kind, way, step).start()
-
-    last = n_dp - 1
-    totals = []
-    for kind, way in streams:
-        ring_copy(kind, way, last - 1).wait_recv()
-        totals.append(slots[kind, way, last].astype(F32) + own(kind, way, me))
-    grad_up_ref[0] = jnp.concatenate(totals[0:2], axis=0).T
-    grad_down_ref[0] = (jnp.concatenate(totals[2:4], axis=0) * my_gain).T
+            forward(kind, way, step)
+
+    for kind, way in streams[0:2]:
+        forward(kind, way, far - 1)
+
+    sums = []
+    for kind in (0, 1):
+        for half in (0, 1):
+            total = own(kind, half, me)
+            for way in (1 - kind, kind):
+                ring_copy(kind, way, half, reach[way, kind] - 1).wait_recv()
+                total += slots[kind, way, half, reach[way, kind]].astype(F32)
+            sums.append(total)
+    for half in (0, 1):
+        rows = slice(half * half_rank, (half + 1) * half_rank)
+        grad_up_ref[0, rows, :] = sums[half]
+        grad_down_ref[0, rows, :] = sums[2 + half] * my_gain
 
     groups = live // group
 
@@ -358,10 +411,11 @@
                 slot = lax.rem(me + (n_dp - hop if way == 0 else hop), n_dp)
                 gather_copy(slot, half, way).wait_send()
 
-    @pl.loop(0, n_dp - 1)
-    def _(step):
-        for kind, way in streams:
-            ring_copy(kind, way, step).wait_send()
+    for kind, way in streams:
+        @pl.loop(0, reach[way, kind])
+        def _(step):
+            for half in (0, 1):
+                ring_copy(kind, way, half, step).wait_send()
 
 
 def solution(mesh):
@@ -369,7 +423,8 @@
 
     def body(activations, norm_gain, adapter_down, adapter_up, counts, upstream):
         raw_rows, width = activations.shape[1:]
-        shard, rank = adapter_down.shape[1:]
+        down_t, up_t = jnp.swapaxes(adapter_down, 1, 2), jnp.swapaxes(adapter_up, 1, 2)
+        rank, shard = down_t.shape[1:]
         live = upstream.shape[0]
         cap = raw_rows // counts.shape[1]
         blocks = live // ROWS
@@ -381,16 +436,19 @@
         dma = pltpu.SemaphoreType.DMA
         vmem = pl.BlockSpec(memory_space=pltpu.VMEM)
         hbm = pl.BlockSpec(memory_space=pl.ANY)
-        return pl.pallas_call(
+        input_grad, grad_down, grad_up = pl.pallas_call(
             functools.partial(kernel, n_sec, n_dp, cap),
             out_shape=(
                 jax.ShapeDtypeStruct((live, columns), BF16),
-                jax.ShapeDtypeStruct((1, shard, rank), F32),
-                jax.ShapeDtypeStruct((1, shard, rank), F32),
+                jax.ShapeDtypeStruct((1, rank, shard), F32),
+                jax.ShapeDtypeStruct((1, rank, shard), F32),
             ),
-            in_specs=[pl.BlockSpec(memory_space=pltpu.SMEM), hbm, vmem, vmem, vmem, hbm],
+            in_specs=[hbm] * 6,
             out_specs=(vmem, vmem, vmem),
             scratch_shapes=[
+                pltpu.SMEM(counts.shape, jnp.int32),
+                pltpu.VMEM((1, width), F32),
+                pltpu.VMEM((2, rank, shard), BF16),
                 pltpu.VMEM((raw_rows, width), BF16),
                 pltpu.VMEM((live, width), BF16),
                 pltpu.VMEM((live, columns), BF16),
@@ -406,21 +464,22 @@
                 pltpu.VMEM((blocks, TILE, wide), BF16),
                 pltpu.VMEM((wide, span), F32),
                 pltpu.VMEM((wide, span), F32),
-                pltpu.VMEM((2, 2, n_dp, rank // 2, shard), BF16),
-                dma((2,)),
+                pltpu.VMEM((2, 2, 2, n_dp // 2 + 1, rank // 2, shard), BF16),
+                dma((6,)),
                 dma((2, 2, n_dp)),
                 dma((2, n_dp)),
                 dma((blocks,)),
                 dma((blocks,)),
                 dma((groups, n_sec)),
                 dma((groups,)),
-                dma((2, 2, n_dp)),
-                dma((2, 2, n_dp)),
+                dma((2, 2, 2, n_dp // 2 + 1)),
+                dma((2, 2, 2, n_dp // 2 + 1)),
             ],
             compiler_params=pltpu.CompilerParams(
-                collective_id=0, has_side_effects=True, vmem_limit_bytes=48 * 1024 * 1024
+                collective_id=0, has_side_effects=True, vmem_limit_bytes=63 * 1024 * 1024
             ),
-        )(counts, activations, norm_gain, adapter_down, adapter_up, upstream)
+        )(counts, activations, norm_gain, down_t, up_t, upstream)
+        return input_grad, jnp.swapaxes(grad_down, 1, 2), jnp.swapaxes(grad_up, 1, 2)
 
     return jax.shard_map(
         body,

time: 219 us -> 191 us (0.87)
  Pallas kernels: 209 us -> 186 us
  local copies, waits for them, and re-layouts: 8.49 us -> 4.56 us
    pallas_call x1, Pallas kernels: 209 us -> 186 us  [body(): pl.pallas_call(functools.partial(kernel, n_sec, n_dp, cap), out_shape=(ja...]
    unnamed x11 -> x3, local copies, waits for them, and re-layouts: 6.94 us -> 4.56 us
where the time goes in v2:
time: 191 us
  Pallas kernels  186 us (97%)
  local copies, waits for them, and re-layouts  4.56 us (2%)
    pallas_call x1, Pallas kernels, body(): pl.pallas_call(functools.partial(kernel, n_sec, n_dp, cap), out_shape=(ja...  186 us
    unnamed x3, local copies, waits for them, and re-layouts  4.56 us

profile of v2, /device:TPU:32, one launch (start us, length us, event | category | flops | bytes accessed | tf_op | source)
XLA Modules:
  0.0 191.0 jit_solution(10337088072772591642)
XLA Ops:
  0.6 185.8 %shard_map.85 = (bf16[96,256]{1,0:T(8,128)(2,1)}, f32[1,64,512]{2,1,0:T(8,128)}, f32[1,64,512]{2,1,0:T(8,128)}) custom-call(s32[1,4]{1,0:T(1,128)} %counts_hbm.1, bf16[1,128,8192]{2,1,0:T(8,128)(2,1)} %x_hbm.1, f32[1,8192]{1,0:T(1,128)} %gain_hbm.1, bf16[1,64,512]{2,1,0:T(8,128)(2,1)} %bitcast.6, bf16[1,64,512]{2,1,0:T(8,128)(2,1)} %bitcast.7, ...), custom_call_target="tpu_custom_call" | custom-call | tf_op jit(solution)/shard_map/pallas_call | solution.py:439
  186.5 1.4 copy.12
  187.9 1.6 copy.13
  189.5 1.6 copy.14

commit v3 on v2

v3 whole, which is shorter than its diff:
```python
import functools

import jax
import jax.numpy as jnp
from jax import lax
from jax.experimental import pallas as pl
from jax.experimental.pallas import tpu as pltpu
from jax.sharding import PartitionSpec as P

ALPHA = 2.0
EPS = 1e-05
QUARTERS = 4
TILE = 16
ROWS = TILE // QUARTERS
MESH = pl.DeviceIdType.MESH
F32 = jnp.float32
BF16 = jnp.bfloat16


def iota(shape, dim):
    return lax.broadcasted_iota(jnp.int32, shape, dim)


def quarter_mask(shape, rank):
    quarter = (iota(shape, 0) // ROWS) % QUARTERS
    return quarter == iota(shape, 1) // rank


def dot(a, b, dims=((1,), (0,)), **kw):
    return lax.dot_general(a, b, (dims, ((), ())), preferred_element_type=F32, **kw)


def kernel(
    n_sec, n_dp, cap,
    counts_hbm, x_hbm, gain_hbm, down_hbm, up_hbm, upstream_hbm,
    input_grad_ref, grad_down_ref, grad_up_ref,
    counts_ref, gain_ref, own_maps, raw, nat, landed, pieces, weight_up, weight_down,
    held_x, row_scale, other_x, other_scale, coef_rank, projected_all,
    gin, gout, lowered_all, part_up, part_down, lent, borrowed, slots,
    load_sem, gather_send, gather_recv, share_send, share_recv, swap_send, swap_recv,
    chain_send, chain_recv, lend_send, lend_recv, final_send, final_recv, ring_send, ring_recv,
):
    sec, me = lax.axis_index("section"), lax.axis_index("dp")
    right, left = lax.rem(me + 1, n_dp), lax.rem(me + n_dp - 1, n_dp)
    core = lax.rem(sec, 2)
    other = 1 - core
    mate = sec + 1 - 2 * core
    half_rows, width = nat.shape
    live = 2 * half_rows
    blocks = half_rows // ROWS
    packed = blocks * TILE
    span = width // QUARTERS
    rank, shard = down_hbm.shape[1:]
    per_quarter = span // shard
    columns = width // n_sec
    wide = QUARTERS * rank
    far = n_dp // 2
    is_top, is_end = sec >= n_sec - 2, sec < 2

    small = [
        pltpu.make_async_copy(up_hbm, own_maps.at[pl.ds(0, 1)], load_sem.at[2]),
        pltpu.make_async_copy(down_hbm, own_maps.at[pl.ds(1, 1)], load_sem.at[3]),
        pltpu.make_async_copy(gain_hbm, gain_ref, load_sem.at[4]),
        pltpu.make_async_copy(counts_hbm, counts_ref, load_sem.at[5]),
    ]
    for load in small:
        load.start()
    load_x = pltpu.make_async_copy(x_hbm.at[0], raw, load_sem.at[0])
    load_x.start()
    my_half = pl.ds(pl.multiple_of(core * half_rows, half_rows), half_rows)
    load_up = pltpu.make_async_copy(upstream_hbm.at[my_half], nat, load_sem.at[1])

    @pl.when(is_top)
    def _():
        load_up.start()

    barrier = pltpu.get_barrier_semaphore()

    def greet(**where):
        pl.semaphore_signal(barrier, inc=1, device_id=where, device_id_type=MESH)

    greet(dp=left)
    greet(dp=right)
    greet(section=mate)

    @pl.when(sec >= 2)
    def _():
        greet(section=sec - 2)

    @pl.when(sec < n_sec - 2)
    def _():
        greet(section=sec + 2)

    for end in (0, 1):
        @pl.when((sec >= 2) & (sec != end + 2))
        def _():
            greet(section=end)

    @pl.when(is_end)
    def _():
        @pl.loop(2, n_sec)
        def _(c):
            @pl.when(c != sec + 2)
            def _():
                greet(section=c)

    for load in small:
        load.wait()
    my_gain = gain_ref[:, pl.ds(pl.multiple_of(me * shard, shard), shard)]
    pieces[core, me, 0:rank, :] = own_maps[0]
    pieces[core, me, rank:2 * rank, :] = (own_maps[1].astype(F32) * my_gain).astype(BF16)

    def greeted(when, amount):
        @pl.when(when)
        def _():
            pl.semaphore_wait(barrier, amount)

    near_end = (sec >= 2) & (sec < 4)
    greeted(is_end, 3 + 1 + n_sec - 3)
    if n_sec > 4:
        greeted(near_end, 3 + 2 + 1)
        greeted((sec >= 4) & (sec < n_sec - 2), 3 + 2 + 2)
        greeted(is_top, 3 + 1 + 2)
    else:
        greeted(near_end, 3 + 1 + 1)

    def gather_copy(slot, half, way):
        part = pieces.at[core, slot, pl.ds(half * rank, rank)]
        return pltpu.make_async_remote_copy(
            src_ref=part,
            dst_ref=part,
            send_sem=gather_send.at[way, half, slot],
            recv_sem=gather_recv.at[half, slot],
            device_id={"dp": right if way == 0 else left},
            device_id_type=MESH,
        )

    def to_mate(source, target, send_sem, recv_sem):
        return pltpu.make_async_remote_copy(
            src_ref=source,
            dst_ref=target,
            send_sem=send_sem,
            recv_sem=recv_sem,
            device_id={"section": mate},
            device_id_type=MESH,
        )

    def share_copy(parity, slot, half):
        part = pieces.at[parity, slot, pl.ds(half * rank, rank)]
        return to_mate(part, part, share_send.at[half, slot], share_recv.at[half, slot])

    def scale_copy(parity):
        return to_mate(other_scale, row_scale.at[parity], swap_send.at[0], swap_recv.at[0])

    def x_copy(parity):
        return to_mate(other_x, held_x.at[parity], swap_send.at[1], swap_recv.at[1])

    reach = {(0, 0): far, (0, 1): far - 1, (1, 0): far - 1, (1, 1): far}
    for half in (0, 1):
        for way in (0, 1):
            gather_copy(me, half, way).start()
    for half in (0, 1):
        share_copy(core, me, half).start()

    load_x.wait()
    raw_rows = raw.shape[0]
    members = counts_ref.shape[1]

    def place(parity, slot):
        rows = pl.ds(pl.multiple_of((slot // per_quarter) * rank, rank), rank)
        cols = pl.ds(pl.multiple_of(lax.rem(slot, per_quarter) * shard, shard), shard)
        weight_down[parity, rows, cols] = pieces[parity, slot, rank:2 * rank, :]

    def sources(shape, half):
        line = iota(shape, 0)
        position = half * half_rows + (line // TILE) * ROWS + lax.rem(line, ROWS)
        source = position
        bound = jnp.int32(0)
        for member in range(members - 1):
            count = counts_ref[0, member]
            bound = bound + count
            source = source + jnp.where(position >= bound, cap - count, 0)
        return source == iota(shape, 1), (line // ROWS) % QUARTERS

    prep_rows = 16
    norm_jobs = raw_rows // prep_rows
    inverses = []

    def pack(n, half):
        chosen, quarter = sources((packed, raw_rows), half)
        total = jnp.zeros((packed, shard), F32)
        for q in range(QUARTERS):
            pick = (chosen & (quarter == q)).astype(BF16)
            total += dot(pick, raw[:, q * span + n * shard:q * span + (n + 1) * shard])
        return total.astype(BF16).reshape(blocks, TILE, shard)

    def work(job):
        if job < norm_jobs:
            rows = pl.ds(job * prep_rows, prep_rows)
            values = raw[rows, :].astype(F32)
            inverse = lax.rsqrt(jnp.mean(values * values, axis=-1, keepdims=True) + EPS)
            raw[rows, :] = (values * inverse).astype(BF16)
            inverses.append(inverse)
        elif job == norm_jobs:
            inverse_all = jnp.broadcast_to(jnp.concatenate(inverses, axis=0), (raw_rows, 128))
            for half in (other, core):
                chosen, _ = sources((packed, raw_rows), half)
                scale = dot(chosen.astype(F32), inverse_all, precision=lax.Precision.HIGHEST)
                scale = scale.reshape(blocks, TILE, 128)
                if half is other:
                    other_scale[...] = scale
                    scale_copy(core).start()
                else:
                    row_scale[core] = scale
        elif job <= norm_jobs + per_quarter:
            n = job - norm_jobs - 1
            other_x[:, :, n * shard:(n + 1) * shard] = pack(n, other)
            if n == per_quarter - 1:
                x_copy(core).start()
        elif job <= norm_jobs + 2 * per_quarter:
            n = job - norm_jobs - 1 - per_quarter
            held_x[core, :, :, n * shard:(n + 1) * shard] = pack(n, core)

    jobs = norm_jobs + 1 + 2 * per_quarter
    done = 0
    turns = 2 * far
    turn = 0

    def from_mate(hop):
        for slot in [me] if hop == 0 else [lax.rem(me + n_dp - hop, n_dp), lax.rem(me + hop, n_dp)]:
            for half in (0, 1):
                share_copy(other, slot, half).wait_recv()
            place(other, slot)
            if hop == far:
                break

    place(core, me)
    for hop in range(1, far + 1):
        for half in (0, 1):
            for way in (0, 1):
                if hop <= reach[way, half]:
                    slot = lax.rem(me + (n_dp - hop if way == 0 else hop), n_dp)
                    here = gather_copy(slot, half, way)
                    here.wait_recv()
                    if hop < reach[way, half]:
                        here.start()
                    share_copy(core, slot, half).start()
                    if half == 1:
                        place(core, slot)
            turn += 1
            while done * turns < jobs * turn:
                work(done)
                done += 1
        from_mate(hop - 1)

    @pl.when(is_top)
    def _():
        load_up.wait()
        line = iota((packed, half_rows), 0)
        position = (line // TILE) * ROWS + lax.rem(line, ROWS)
        chosen = position == iota((packed, half_rows), 1)
        quarter = (line // ROWS) % QUARTERS
        for n in range(per_quarter):
            cols = slice(n * shard, (n + 1) * shard)
            total = jnp.zeros((packed, shard), F32)
            for q in range(QUARTERS):
                pick = (chosen & (quarter == q)).astype(BF16)
                total += dot(pick, nat[:, q * span + n * shard:q * span + (n + 1) * shard])
            gin[1, :, :, cols] = total.astype(BF16).reshape(blocks, TILE, shard)

    from_mate(far)
    scale_copy(other).wait_recv()
    x_copy(other).wait_recv()

    for parity in (1, 0):
        for n in range(per_quarter):
            stack = [pieces[parity, q * per_quarter + n, 0:rank, :] for q in range(QUARTERS)]
            weight_up[parity, n * shard:(n + 1) * shard, :] = jnp.concatenate(stack, axis=0).T

    def fold(product):
        pair = product[:, 0:128] + product[:, 128:256]
        return pair + pltpu.roll(pair, 64, 1)

    for parity in (1, 0):
        product = dot(held_x[parity].reshape(packed, span), weight_down[parity], ((1,), (1,)))
        product = jnp.where(quarter_mask((packed, wide), rank), product, 0.0)
        folded = fold(product).reshape(blocks, TILE, 128)
        folded = folded[:, 0:8, :] + folded[:, 8:16, :]
        folded = (folded + pltpu.roll(folded, 4, 1)).astype(BF16).astype(F32)
        lane = lax.broadcasted_iota(jnp.int32, folded.shape, 2)
        coef_rank[parity] = jnp.where(lane < rank, folded * (1.0 / width), 0.0)
        tall = jnp.concatenate([folded, folded], axis=1)
        tall = jnp.concatenate([tall, tall], axis=2).reshape(packed, wide)
        projected_all[parity] = jnp.where(quarter_mask((packed, wide), rank), tall, 0.0).astype(BF16)

    def chain_copy(block):
        return pltpu.make_async_remote_copy(
            src_ref=gout.at[block],
            dst_ref=gin.at[1, block],
            send_sem=chain_send.at[block],
            recv_sem=chain_recv.at[block],
            device_id={"section": lax.rem(sec + n_sec - 2, n_sec)},
            device_id_type=MESH,
        )

    group = 16
    group_blocks = group // ROWS
    groups = half_rows // group

    def final_copy(half, k, c):
        rows = pl.ds(pl.multiple_of(k * group, group), group)
        return pltpu.make_async_remote_copy(
            src_ref=nat.at[rows, pl.ds(pl.multiple_of(c * columns, columns), columns)],
            dst_ref=landed.at[pl.ds(pl.multiple_of(half * half_rows + k * group, group), group)],
            send_sem=final_send.at[k, c],
            recv_sem=final_recv.at[half, k],
            device_id={"section": c},
            device_id_type=MESH,
        )

    mask = quarter_mask((TILE, wide), rank)

    def spread(rows8):
        tall = jnp.concatenate([rows8, rows8], axis=0)
        tall = jnp.concatenate([tall, tall], axis=1)
        return jnp.where(mask, tall, 0.0).astype(BF16)

    def unpack(block):
        k = block // group_blocks
        finished = gout[pl.ds(k * group_blocks, group_blocks)].reshape(group_blocks * TILE, span)
        shape = (group, group_blocks * TILE)
        row = iota(shape, 0)
        rows = pl.ds(pl.multiple_of(k * group, group), group)
        for q in range(QUARTERS):
            want = (row // ROWS) * TILE + q * ROWS + lax.rem(row, ROWS)
            pick = (want == iota(shape, 1)).astype(BF16)
            nat[rows, q * span:(q + 1) * span] = dot(pick, finished).astype(BF16)

        @pl.loop(0, n_sec)
        def _(c):
            @pl.when(c != sec)
            def _():
                final_copy(core, k, c).start()

    def layer(parity, block, result):
        values = gin[parity, block]
        product = dot(values, weight_up[parity])
        pair = fold(jnp.where(mask, product, 0.0))
        pair = pair[0:8, :] + pair[8:16, :]
        lowered = ((pair + pltpu.roll(pair, 4, 0)) * ALPHA).astype(BF16).astype(F32)
        scaled = lowered * row_scale[parity, block, 0:8, :]
        coef = jnp.sum(scaled * coef_rank[parity, block], axis=-1, keepdims=True)
        coef = jnp.concatenate([coef, coef], axis=0)
        back = dot(spread(scaled), weight_down[parity])
        fresh = values.astype(F32) + (back - held_x[parity, block].astype(F32) * coef)
        result[...] = fresh.astype(BF16)
        return lowered

    def run_chain(receives, sends):
        @pl.loop(0, blocks)
        def _(block):
            if receives:
                chain_copy(block).wait_recv()
            first = layer(1, block, gin.at[0, block])
            second = layer(0, block, gout.at[block])
            if sends:
                chain_copy(block).start()
            lowered_all[1, block] = spread(first)
            lowered_all[0, block] = spread(second)
            if not sends:
                @pl.when(lax.rem(block, group_blocks) == group_blocks - 1)
                def _():
                    unpack(block)

    @pl.when(is_top)
    def _():
        run_chain(False, True)

    if n_sec > 4:
        @pl.when((sec >= 2) & (sec < n_sec - 2))
        def _():
            run_chain(True, True)

    @pl.when(is_end)
    def _():
        run_chain(True, False)

    half_rank = rank // 2
    parts = (part_up, part_down)
    offsets = (0, -1, 1, 2)[:per_quarter]

    def chunk_at(offset):
        return lax.rem(me + far + per_quarter + offset, per_quarter)

    def flip(values):
        return values.astype(F32).T.astype(BF16)

    def lend_copy(kind, n):
        return to_mate(
            lent.at[kind, n], borrowed.at[kind, n], lend_send.at[kind, n], lend_recv.at[kind, n]
        )

    def products(parity, n):
        cols = pl.ds(pl.multiple_of(n * shard, shard), shard)
        up = dot(flipped[parity is core][0], gin[parity, :, :, cols].reshape(packed, shard))
        down = dot(flipped[parity is core][1], held_x[parity, :, :, cols].reshape(packed, shard))
        return cols, up * (ALPHA / live), down * (1.0 / live)

    flipped = {
        parity is core: (flip(projected_all[parity]), flip(lowered_all[parity].reshape(packed, wide)))
        for parity in (other, core)
    }
    for offset in offsets:
        n = chunk_at(offset)
        _, up, down = products(other, n)
        lent[0, n] = up.astype(BF16)
        lend_copy(0, n).start()
        lent[1, n] = down.astype(BF16)
        lend_copy(1, n).start()

    def partial(offset):
        if offset not in offsets:
            return
        n = chunk_at(offset)
        cols, up, down = products(core, n)
        for kind in (0, 1):
            lend_copy(kind, n).wait_recv()
        part_up[:, cols] = up + borrowed[0, n].astype(F32)
        part_down[:, cols] = down + borrowed[1, n].astype(F32)

    def own(kind, half, piece):
        start = (piece // per_quarter) * rank + half * half_rank
        rows = pl.ds(pl.multiple_of(start, half_rank), half_rank)
        cols = pl.ds(pl.multiple_of(lax.rem(piece, per_quarter) * shard, shard), shard)
        return parts[kind][rows, cols]

    def ring_copy(kind, way, half, step):
        return pltpu.make_async_remote_copy(
            src_ref=slots.at[kind, way, half, step],
            dst_ref=slots.at[kind, way, half, step + 1],
            send_sem=ring_send.at[kind, way, half, step],
            recv_sem=ring_recv.at[kind, way, half, step + 1],
            device_id={"dp": right if way == 0 else left},
            device_id_type=MESH,
        )

    def target(kind, way, step):
        distance = reach[way, kind] - step
        return lax.rem(me + (distance if way == 0 else n_dp - distance), n_dp)

    def begin(kind, way):
        for half in (0, 1):
            slots[kind, way, half, 0] = own(kind, half, target(kind, way, 0)).astype(BF16)
            ring_copy(kind, way, half, 0).start()

    def forward(kind, way, step):
        for half in (0, 1):
            ring_copy(kind, way, half, step - 1).wait_recv()
            total = slots[kind, way, half, step].astype(F32) + own(kind, half, target(kind, way, step))
            slots[kind, way, half, step] = total.astype(BF16)
            ring_copy(kind, way, half, step).start()

    partial(0)
    begin(0, 0)
    begin(1, 1)
    partial(-1)
    begin(1, 0)
    partial(1)
    begin(0, 1)
    partial(2)
    streams = [(0, 0), (1, 1), (1, 0), (0, 1)]

    @pl.loop(1, far - 1)
    def _(step):
        for kind, way in streams:
            forward(kind, way, step)

    for kind, way in streams[0:2]:
        forward(kind, way, far - 1)

    sums = []
    for kind in (0, 1):
        for half in (0, 1):
            total = own(kind, half, me)
            for way in (1 - kind, kind):
                ring_copy(kind, way, half, reach[way, kind] - 1).wait_recv()
                total += slots[kind, way, half, reach[way, kind]].astype(F32)
            sums.append(total)
    for half in (0, 1):
        rows = slice(half * half_rank, (half + 1) * half_rank)
        grad_up_ref[0, rows, :] = sums[half]
        grad_down_ref[0, rows, :] = sums[2 + half] * my_gain

    for end in (0, 1):
        @pl.when(sec != end)
        def _():
            @pl.loop(0, groups)
            def _(k):
                final_copy(end, k, sec).wait_recv()

    input_grad_ref[...] = landed[...]

    @pl.when(is_end)
    def _():
        input_grad_ref[my_half, :] = nat[:, pl.ds(pl.multiple_of(sec * columns, columns), columns)]

        @pl.loop(0, groups)
        def _(k):
            @pl.loop(0, n_sec)
            def _(c):
                @pl.when(c != sec)
                def _():
                    final_copy(core, k, c).wait_send()

    @pl.when(sec >= 2)
    def _():
        @pl.loop(0, blocks)
        def _(block):
            chain_copy(block).wait_send()

    for half in (0, 1):
        for way in (0, 1):
            for hop in range(reach[way, half]):
                slot = lax.rem(me + (n_dp - hop if way == 0 else hop), n_dp)
                gather_copy(slot, half, way).wait_send()
        @pl.loop(0, n_dp)
        def _(slot):
            share_copy(core, slot, half).wait_send()

    scale_copy(core).wait_send()
    x_copy(core).wait_send()
    for kind in (0, 1):
        for n in range(per_quarter):
            lend_copy(kind, n).wait_send()
    for kind, way in streams:
        @pl.loop(0, reach[way, kind])
        def _(step):
            for half in (0, 1):
                ring_copy(kind, way, half, step).wait_send()


def solution(mesh):
    n_sec, n_dp = mesh.shape["section"], mesh.shape["dp"]

    def body(activations, norm_gain, adapter_down, adapter_up, counts, upstream):
        raw_rows, width = activations.shape[1:]
        down_t, up_t = jnp.swapaxes(adapter_down, 1, 2), jnp.swapaxes(adapter_up, 1, 2)
        rank, shard = down_t.shape[1:]
        live = upstream.shape[0]
        half_rows = live // 2
        cap = raw_rows // counts.shape[1]
        blocks = half_rows // ROWS
        packed = blocks * TILE
        span = width // QUARTERS
        wide = QUARTERS * rank
        columns = width // n_sec
        per_quarter = span // shard
        groups = half_rows // 16
        far = n_dp // 2
        dma = pltpu.SemaphoreType.DMA
        vmem = pl.BlockSpec(memory_space=pltpu.VMEM)
        hbm = pl.BlockSpec(memory_space=pl.ANY)
        input_grad, grad_down, grad_up = pl.pallas_call(
            functools.partial(kernel, n_sec, n_dp, cap),
            out_shape=(
                jax.ShapeDtypeStruct((live, columns), BF16),
                jax.ShapeDtypeStruct((1, rank, shard), F32),
                jax.ShapeDtypeStruct((1, rank, shard), F32),
            ),
            in_specs=[hbm] * 6,
            out_specs=(vmem, vmem, vmem),
            scratch_shapes=[
                pltpu.SMEM(counts.shape, jnp.int32),
                pltpu.VMEM((1, width), F32),
                pltpu.VMEM((2, rank, shard), BF16),
                pltpu.VMEM((raw_rows, width), BF16),
                pltpu.VMEM((half_rows, width), BF16),
                pltpu.VMEM((live, columns), BF16),
                pltpu.VMEM((2, n_dp, 2 * rank, shard), BF16),
                pltpu.VMEM((2, span, wide), BF16),
                pltpu.VMEM((2, wide, span), BF16),
                pltpu.VMEM((2, blocks, TILE, span), BF16),
                pltpu.VMEM((2, blocks, TILE, 128), F32),
                pltpu.VMEM((blocks, TILE, span), BF16),
                pltpu.VMEM((blocks, TILE, 128), F32),
                pltpu.VMEM((2, blocks, 8, 128), F32),
                pltpu.VMEM((2, packed, wide), BF16),
                pltpu.VMEM((2, blocks, TILE, span), BF16),
                pltpu.VMEM((blocks, TILE, span), BF16),
                pltpu.VMEM((2, blocks, TILE, wide), BF16),
                pltpu.VMEM((wide, span), F32),
                pltpu.VMEM((wide, span), F32),
                pltpu.VMEM((2, per_quarter, wide, shard), BF16),
                pltpu.VMEM((2, per_quarter, wide, shard), BF16),
                pltpu.VMEM((2, 2, 2, far + 1, rank // 2, shard), BF16),
                dma((6,)),
                dma((2, 2, n_dp)),
                dma((2, n_dp)),
                dma((2, n_dp)),
                dma((2, n_dp)),
                dma((2,)),
                dma((2,)),
                dma((blocks,)),
                dma((blocks,)),
                dma((2, per_quarter)),
                dma((2, per_quarter)),
                dma((groups, n_sec)),
                dma((2, groups)),
                dma((2, 2, 2, far + 1)),
                dma((2, 2, 2, far + 1)),
            ],
            compiler_params=pltpu.CompilerParams(
                collective_id=0, has_side_effects=True, vmem_limit_bytes=63 * 1024 * 1024
            ),
        )(counts, activations, norm_gain, down_t, up_t, upstream)
        return input_grad, jnp.swapaxes(grad_down, 1, 2), jnp.swapaxes(grad_up, 1, 2)

    return jax.shard_map(
        body,
        mesh=mesh,
        in_specs=(
            P("section", "dp", None),
            P("section", None),
            P("section", "dp", None),
            P("section", "dp", None),
            P("dp", None),
            P("dp", None),
        ),
        out_specs=(P("dp", "section"), P("section", "dp", None), P("section", "dp", None)),
        check_vma=False,
    )
```

time: 191 us -> 184 us (0.963)
  Pallas kernels: 186 us -> 178 us
    pallas_call x1, Pallas kernels: 186 us -> 178 us  [body(): pl.pallas_call(functools.partial(kernel, n_sec, n_dp, cap), out_shape=(ja...]
where the time goes in v3:
time: 184 us
  Pallas kernels  178 us (97%)
  local copies, waits for them, and re-layouts  4.56 us (2%)
    pallas_call x1, Pallas kernels, body(): pl.pallas_call(functools.partial(kernel, n_sec, n_dp, cap), out_shape=(ja...  178 us
    unnamed x3, local copies, waits for them, and re-layouts  4.56 us

profile of v3, /device:TPU:32, one launch (start us, length us, event | category | flops | bytes accessed | tf_op | source)
XLA Modules:
  0.0 183.5 jit_solution(5512625468574871609)
XLA Ops:
  0.6 178.3 %shard_map.85 = (bf16[96,256]{1,0:T(8,128)(2,1)}, f32[1,64,512]{2,1,0:T(8,128)}, f32[1,64,512]{2,1,0:T(8,128)}) custom-call(s32[1,4]{1,0:T(1,128)} %counts_hbm.1, bf16[1,128,8192]{2,1,0:T(8,128)(2,1)} %x_hbm.1, f32[1,8192]{1,0:T(1,128)} %gain_hbm.1, bf16[1,64,512]{2,1,0:T(8,128)(2,1)} %bitcast.6, bf16[1,64,512]{2,1,0:T(8,128)(2,1)} %bitcast.7, ...), custom_call_target="tpu_custom_call" | custom-call | tf_op jit(solution)/shard_map/pallas_call | solution.py:563
  179.0 1.4 copy.12
  180.4 1.6 copy.13
  182.0 1.6 copy.14

commit v4 on v3

--- a/solution.py
+++ b/solution.py
@@ -10,6 +10,7 @@
 ALPHA = 2.0
 EPS = 1e-05
 QUARTERS = 4
+PARTS = 4
 TILE = 16
 ROWS = TILE // QUARTERS
 MESH = pl.DeviceIdType.MESH
@@ -36,7 +37,7 @@
     input_grad_ref, grad_down_ref, grad_up_ref,
     counts_ref, gain_ref, own_maps, raw, nat, landed, pieces, weight_up, weight_down,
     held_x, row_scale, other_x, other_scale, coef_rank, projected_all,
-    gin, gout, lowered_all, part_up, part_down, lent, borrowed, slots,
+    gin, gout, lowered_all, projected_t, part_up, part_down, lent, borrowed, slots,
     load_sem, gather_send, gather_recv, share_send, share_recv, swap_send, swap_recv,
     chain_send, chain_recv, lend_send, lend_recv, final_send, final_recv, ring_send, ring_recv,
 ):
@@ -96,14 +97,6 @@
         def _():
             greet(section=end)
 
-    @pl.when(is_end)
-    def _():
-        @pl.loop(2, n_sec)
-        def _(c):
-            @pl.when(c != sec + 2)
-            def _():
-                greet(section=c)
-
     for load in small:
         load.wait()
     my_gain = gain_ref[:, pl.ds(pl.multiple_of(me * shard, shard), shard)]
@@ -115,22 +108,20 @@
         def _():
             pl.semaphore_wait(barrier, amount)
 
-    near_end = (sec >= 2) & (sec < 4)
     greeted(is_end, 3 + 1 + n_sec - 3)
     if n_sec > 4:
-        greeted(near_end, 3 + 2 + 1)
-        greeted((sec >= 4) & (sec < n_sec - 2), 3 + 2 + 2)
-        greeted(is_top, 3 + 1 + 2)
-    else:
-        greeted(near_end, 3 + 1 + 1)
-
-    def gather_copy(slot, half, way):
-        part = pieces.at[core, slot, pl.ds(half * rank, rank)]
+        greeted((sec >= 2) & (sec < n_sec - 2), 3 + 2)
+    greeted(is_top, 3 + 1)
+
+    cut = 2 * rank // PARTS
+
+    def gather_copy(slot, part, way):
+        span_rows = pieces.at[core, slot, pl.ds(part * cut, cut)]
         return pltpu.make_async_remote_copy(
-            src_ref=part,
-            dst_ref=part,
-            send_sem=gather_send.at[way, half, slot],
-            recv_sem=gather_recv.at[half, slot],
+            src_ref=span_rows,
+            dst_ref=span_rows,
+            send_sem=gather_send.at[way, part, slot],
+            recv_sem=gather_recv.at[part, slot],
             device_id={"dp": right if way == 0 else left},
             device_id_type=MESH,
         )
@@ -145,9 +136,9 @@
             device_id_type=MESH,
         )
 
-    def share_copy(parity, slot, half):
-        part = pieces.at[parity, slot, pl.ds(half * rank, rank)]
-        return to_mate(part, part, share_send.at[half, slot], share_recv.at[half, slot])
+    def share_copy(parity, slot):
+        piece = pieces.at[parity, slot]
+        return to_mate(piece, piece, share_send.at[slot], share_recv.at[slot])
 
     def scale_copy(parity):
         return to_mate(other_scale, row_scale.at[parity], swap_send.at[0], swap_recv.at[0])
@@ -156,11 +147,11 @@
         return to_mate(other_x, held_x.at[parity], swap_send.at[1], swap_recv.at[1])
 
     reach = {(0, 0): far, (0, 1): far - 1, (1, 0): far - 1, (1, 1): far}
-    for half in (0, 1):
+    half_of = [2 * part // PARTS for part in range(PARTS)]
+    for part in range(PARTS):
         for way in (0, 1):
-            gather_copy(me, half, way).start()
-    for half in (0, 1):
-        share_copy(core, me, half).start()
+            gather_copy(me, part, way).start()
+    share_copy(core, me).start()
 
     load_x.wait()
     raw_rows = raw.shape[0]
@@ -223,29 +214,28 @@
 
     jobs = norm_jobs + 1 + 2 * per_quarter
     done = 0
-    turns = 2 * far
+    turns = PARTS * far
     turn = 0
 
     def from_mate(hop):
         for slot in [me] if hop == 0 else [lax.rem(me + n_dp - hop, n_dp), lax.rem(me + hop, n_dp)]:
-            for half in (0, 1):
-                share_copy(other, slot, half).wait_recv()
+            share_copy(other, slot).wait_recv()
             place(other, slot)
             if hop == far:
                 break
 
     place(core, me)
     for hop in range(1, far + 1):
-        for half in (0, 1):
+        for part in range(PARTS):
             for way in (0, 1):
-                if hop <= reach[way, half]:
+                if hop <= reach[way, half_of[part]]:
                     slot = lax.rem(me + (n_dp - hop if way == 0 else hop), n_dp)
-                    here = gather_copy(slot, half, way)
+                    here = gather_copy(slot, part, way)
                     here.wait_recv()
-                    if hop < reach[way, half]:
+                    if hop < reach[way, half_of[part]]:
                         here.start()
-                    share_copy(core, slot, half).start()
-                    if half == 1:
+                    if part == PARTS - 1:
+                        share_copy(core, slot).start()
                         place(core, slot)
             turn += 1
             while done * turns < jobs * turn:
@@ -293,6 +283,19 @@
         tall = jnp.concatenate([tall, tall], axis=2).reshape(packed, wide)
         projected_all[parity] = jnp.where(quarter_mask((packed, wide), rank), tall, 0.0).astype(BF16)
 
+    def flip(values):
+        return values.astype(F32).T.astype(BF16)
+
+    late = is_top & (core == 0)
+
+    def flip_projected():
+        for parity in (0, 1):
+            projected_t[parity] = flip(projected_all[parity])
+
+    @pl.when(jnp.logical_not(late))
+    def _():
+        flip_projected()
+
     def chain_copy(block):
         return pltpu.make_async_remote_copy(
             src_ref=gout.at[block],
@@ -325,8 +328,7 @@
         tall = jnp.concatenate([tall, tall], axis=1)
         return jnp.where(mask, tall, 0.0).astype(BF16)
 
-    def unpack(block):
-        k = block // group_blocks
+    def unpack(k):
         finished = gout[pl.ds(k * group_blocks, group_blocks)].reshape(group_blocks * TILE, span)
         shape = (group, group_blocks * TILE)
         row = iota(shape, 0)
@@ -336,8 +338,17 @@
             pick = (want == iota(shape, 1)).astype(BF16)
             nat[rows, q * span:(q + 1) * span] = dot(pick, finished).astype(BF16)
 
-        @pl.loop(0, n_sec)
-        def _(c):
+    def hand_out(unit):
+        k, late_half = unit // 2, lax.rem(unit, 2)
+
+        @pl.when(late_half == 0)
+        def _():
+            unpack(k)
+
+        @pl.loop(0, n_sec // 2)
+        def _(step):
+            c = late_half * (n_sec // 2) + step
+
             @pl.when(c != sec)
             def _():
                 final_copy(core, k, c).start()
@@ -367,10 +378,6 @@
                 chain_copy(block).start()
             lowered_all[1, block] = spread(first)
             lowered_all[0, block] = spread(second)
-            if not sends:
-                @pl.when(lax.rem(block, group_blocks) == group_blocks - 1)
-                def _():
-                    unpack(block)
 
     @pl.when(is_top)
     def _():
@@ -391,9 +398,6 @@
 
     def chunk_at(offset):
         return lax.rem(me + far + per_quarter + offset, per_quarter)
-
-    def flip(values):
-        return values.astype(F32).T.astype(BF16)
 
     def lend_copy(kind, n):
         return to_mate(
@@ -406,8 +410,12 @@
         down = dot(flipped[parity is core][1], held_x[parity, :, :, cols].reshape(packed, shard))
         return cols, up * (ALPHA / live), down * (1.0 / live)
 
+    @pl.when(late)
+    def _():
+        flip_projected()
+
     flipped = {
-        parity is core: (flip(projected_all[parity]), flip(lowered_all[parity].reshape(packed, wide)))
+        parity is core: (projected_t[parity], flip(lowered_all[parity].reshape(packed, wide)))
         for parity in (other, core)
     }
     for offset in offsets:
@@ -470,10 +478,25 @@
     partial(2)
     streams = [(0, 0), (1, 1), (1, 0), (0, 1)]
 
+    units = 2 * groups
+    per_step = units // (far - 2) if far > 2 and units % (far - 2) == 0 else 0
+
     @pl.loop(1, far - 1)
     def _(step):
         for kind, way in streams:
             forward(kind, way, step)
+
+        @pl.when(is_end)
+        def _():
+            for extra in range(per_step):
+                hand_out((step - 1) * per_step + extra)
+
+    if per_step == 0:
+        @pl.when(is_end)
+        def _():
+            @pl.loop(0, units)
+            def _(unit):
+                hand_out(unit)
 
     for kind, way in streams[0:2]:
         forward(kind, way, far - 1)
@@ -518,14 +541,15 @@
         def _(block):
             chain_copy(block).wait_send()
 
-    for half in (0, 1):
+    for part in range(PARTS):
         for way in (0, 1):
-            for hop in range(reach[way, half]):
+            for hop in range(reach[way, half_of[part]]):
                 slot = lax.rem(me + (n_dp - hop if way == 0 else hop), n_dp)
-                gather_copy(slot, half, way).wait_send()
-        @pl.loop(0, n_dp)
-        def _(slot):
-            share_copy(core, slot, half).wait_send()
+                gather_copy(slot, part, way).wait_send()
+
+    @pl.loop(0, n_dp)
+    def _(slot):
+        share_copy(core, slot).wait_send()
 
     scale_copy(core).wait_send()
     x_copy(core).wait_send()
@@ -588,16 +612,17 @@
                 pltpu.VMEM((2, blocks, TILE, span), BF16),
                 pltpu.VMEM((blocks, TILE, span), BF16),
                 pltpu.VMEM((2, blocks, TILE, wide), BF16),
+                pltpu.VMEM((2, wide, packed), BF16),
                 pltpu.VMEM((wide, span), F32),
                 pltpu.VMEM((wide, span), F32),
                 pltpu.VMEM((2, per_quarter, wide, shard), BF16),
                 pltpu.VMEM((2, per_quarter, wide, shard), BF16),
                 pltpu.VMEM((2, 2, 2, far + 1, rank // 2, shard), BF16),
                 dma((6,)),
-                dma((2, 2, n_dp)),
-                dma((2, n_dp)),
-                dma((2, n_dp)),
-                dma((2, n_dp)),
+                dma((2, PARTS, n_dp)),
+                dma((PARTS, n_dp)),
+                dma((n_dp,)),
+                dma((n_dp,)),
                 dma((2,)),
                 dma((2,)),
                 dma((blocks,)),

time: 184 us -> 180 us (0.978)
  Pallas kernels: 178 us -> 174 us
    pallas_call x1, Pallas kernels: 178 us -> 174 us  [body(): pl.pallas_call(functools.partial(kernel, n_sec, n_dp, cap), out_shape=(ja...]
where the time goes in v4:
time: 180 us; the launch traced here: 179 us
  Pallas kernels  174 us (97%)
  local copies, waits for them, and re-layouts  4.56 us (3%)
    pallas_call x1, Pallas kernels, body(): pl.pallas_call(functools.partial(kernel, n_sec, n_dp, cap), out_shape=(ja...  174 us
    unnamed x3, local copies, waits for them, and re-layouts  4.56 us

profile of v4, /device:TPU:32, one launch (start us, length us, event | category | flops | bytes accessed | tf_op | source)
XLA Modules:
  0.0 179.4 jit_solution(11171859288978027126)
XLA Ops:
  0.6 174.2 %shard_map.85 = (bf16[96,256]{1,0:T(8,128)(2,1)}, f32[1,64,512]{2,1,0:T(8,128)}, f32[1,64,512]{2,1,0:T(8,128)}) custom-call(s32[1,4]{1,0:T(1,128)} %counts_hbm.1, bf16[1,128,8192]{2,1,0:T(8,128)(2,1)} %x_hbm.1, f32[1,8192]{1,0:T(1,128)} %gain_hbm.1, bf16[1,64,512]{2,1,0:T(8,128)(2,1)} %bitcast.6, bf16[1,64,512]{2,1,0:T(8,128)(2,1)} %bitcast.7, ...), custom_call_target="tpu_custom_call" | custom-call | tf_op jit(solution)/shard_map/pallas_call | solution.py:587
  174.8 1.4 copy.12
  176.3 1.6 copy.13
  177.8 1.6 copy.14

commit v5 on v4

--- a/solution.py
+++ b/solution.py
@@ -34,7 +34,7 @@
 def kernel(
     n_sec, n_dp, cap,
     counts_hbm, x_hbm, gain_hbm, down_hbm, up_hbm, upstream_hbm,
-    input_grad_ref, grad_down_ref, grad_up_ref,
+    input_grad_ref, grads_ref,
     counts_ref, gain_ref, own_maps, raw, nat, landed, pieces, weight_up, weight_down,
     held_x, row_scale, other_x, other_scale, coef_rank, projected_all,
     gin, gout, lowered_all, projected_t, part_up, part_down, lent, borrowed, slots,
@@ -296,12 +296,13 @@
     def _():
         flip_projected()
 
-    def chain_copy(block):
+    def chain_copy(block, side):
+        cols = pl.ds(side * (span // 2), span // 2)
         return pltpu.make_async_remote_copy(
-            src_ref=gout.at[block],
-            dst_ref=gin.at[1, block],
-            send_sem=chain_send.at[block],
-            recv_sem=chain_recv.at[block],
+            src_ref=gout.at[block, :, cols],
+            dst_ref=gin.at[1, block, :, cols],
+            send_sem=chain_send.at[block, side],
+            recv_sem=chain_recv.at[block, side],
             device_id={"section": lax.rem(sec + n_sec - 2, n_sec)},
             device_id_type=MESH,
         )
@@ -353,7 +354,7 @@
             def _():
                 final_copy(core, k, c).start()
 
-    def layer(parity, block, result):
+    def layer(parity, block, result, sends):
         values = gin[parity, block]
         product = dot(values, weight_up[parity])
         pair = fold(jnp.where(mask, product, 0.0))
@@ -362,20 +363,24 @@
         scaled = lowered * row_scale[parity, block, 0:8, :]
         coef = jnp.sum(scaled * coef_rank[parity, block], axis=-1, keepdims=True)
         coef = jnp.concatenate([coef, coef], axis=0)
-        back = dot(spread(scaled), weight_down[parity])
-        fresh = values.astype(F32) + (back - held_x[parity, block].astype(F32) * coef)
-        result[...] = fresh.astype(BF16)
+        scaled = spread(scaled)
+        for side in (0, 1):
+            cols = slice(side * (span // 2), (side + 1) * (span // 2))
+            back = dot(scaled, weight_down[parity, :, cols])
+            fresh = values[:, cols].astype(F32) + (back - held_x[parity, block, :, cols].astype(F32) * coef)
+            result[:, cols] = fresh.astype(BF16)
+            if sends:
+                chain_copy(block, side).start()
         return lowered
 
     def run_chain(receives, sends):
         @pl.loop(0, blocks)
         def _(block):
             if receives:
-                chain_copy(block).wait_recv()
-            first = layer(1, block, gin.at[0, block])
-            second = layer(0, block, gout.at[block])
-            if sends:
-                chain_copy(block).start()
+                for side in (0, 1):
+                    chain_copy(block, side).wait_recv()
+            first = layer(1, block, gin.at[0, block], False)
+            second = layer(0, block, gout.at[block], sends)
             lowered_all[1, block] = spread(first)
             lowered_all[0, block] = spread(second)
 
@@ -408,7 +413,7 @@
         cols = pl.ds(pl.multiple_of(n * shard, shard), shard)
         up = dot(flipped[parity is core][0], gin[parity, :, :, cols].reshape(packed, shard))
         down = dot(flipped[parity is core][1], held_x[parity, :, :, cols].reshape(packed, shard))
-        return cols, up * (ALPHA / live), down * (1.0 / live)
+        return cols, up, down
 
     @pl.when(late)
     def _():
@@ -511,8 +516,8 @@
             sums.append(total)
     for half in (0, 1):
         rows = slice(half * half_rank, (half + 1) * half_rank)
-        grad_up_ref[0, rows, :] = sums[half]
-        grad_down_ref[0, rows, :] = sums[2 + half] * my_gain
+        grads_ref[0, rows, :] = sums[half]
+        grads_ref[1, rows, :] = sums[2 + half] * my_gain
 
     for end in (0, 1):
         @pl.when(sec != end)
@@ -539,7 +544,8 @@
     def _():
         @pl.loop(0, blocks)
         def _(block):
-            chain_copy(block).wait_send()
+            for side in (0, 1):
+                chain_copy(block, side).wait_send()
 
     for part in range(PARTS):
         for way in (0, 1):
@@ -584,15 +590,14 @@
         dma = pltpu.SemaphoreType.DMA
         vmem = pl.BlockSpec(memory_space=pltpu.VMEM)
         hbm = pl.BlockSpec(memory_space=pl.ANY)
-        input_grad, grad_down, grad_up = pl.pallas_call(
+        input_grad, grads = pl.pallas_call(
             functools.partial(kernel, n_sec, n_dp, cap),
             out_shape=(
                 jax.ShapeDtypeStruct((live, columns), BF16),
-                jax.ShapeDtypeStruct((1, rank, shard), F32),
-                jax.ShapeDtypeStruct((1, rank, shard), F32),
+                jax.ShapeDtypeStruct((2, rank, shard), F32),
             ),
             in_specs=[hbm] * 6,
-            out_specs=(vmem, vmem, vmem),
+            out_specs=(vmem, vmem),
             scratch_shapes=[
                 pltpu.SMEM(counts.shape, jnp.int32),
                 pltpu.VMEM((1, width), F32),
@@ -625,8 +630,8 @@
                 dma((n_dp,)),
                 dma((2,)),
                 dma((2,)),
-                dma((blocks,)),
-                dma((blocks,)),
+                dma((blocks, 2)),
+                dma((blocks, 2)),
                 dma((2, per_quarter)),
                 dma((2, per_quarter)),
                 dma((groups, n_sec)),
@@ -638,7 +643,8 @@
                 collective_id=0, has_side_effects=True, vmem_limit_bytes=63 * 1024 * 1024
             ),
         )(counts, activations, norm_gain, down_t, up_t, upstream)
-        return input_grad, jnp.swapaxes(grad_down, 1, 2), jnp.swapaxes(grad_up, 1, 2)
+        grads = jnp.swapaxes(grads, 1, 2)
+        return input_grad, grads[1:2] * (1.0 / live), grads[0:1] * (ALPHA / live)
 
     return jax.shard_map(
         body,

time: 180 us -> 177 us (0.983)
  local copies, waits for them, and re-layouts: 4.56 us -> 1.42 us
    unnamed x3 -> x1, local copies, waits for them, and re-layouts: 4.56 us -> 1.42 us
where the time goes in v5:
time: 177 us
  Pallas kernels  173 us (98%)
    pallas_call x1, Pallas kernels, body(): pl.pallas_call(functools.partial(kernel, n_sec, n_dp, cap), out_shape=(ja...  173 us

profile of v5, /device:TPU:32, one launch (start us, length us, event | category | flops | bytes accessed | tf_op | source)
XLA Modules:
  0.0 177.3 jit_solution(13630621336181230980)
XLA Ops:
  0.6 173.5 %shard_map.85 = (bf16[96,256]{1,0:T(8,128)(2,1)}, f32[2,64,512]{2,1,0:T(8,128)}) custom-call(s32[1,4]{1,0:T(1,128)} %counts_hbm.1, bf16[1,128,8192]{2,1,0:T(8,128)(2,1)} %x_hbm.1, f32[1,8192]{1,0:T(1,128)} %gain_hbm.1, bf16[1,64,512]{2,1,0:T(8,128)(2,1)} %bitcast.4, bf16[1,64,512]{2,1,0:T(8,128)(2,1)} %bitcast.5, bf16[96,8192]{1,0:T(8,128)(2,1)} %upstream_hbm.1), custom_call_target="tpu_custom_call" | custom-call | tf_op jit(solution)/shard_map/pallas_call | solution.py:593
  174.1 1.7 slice_multiply_fusion
  175.8 1.4 copy.10
